TPU v7x, 32 devices: a whole 2x2x4 slice. The times are simulated.
32 devices in a mesh: seq: 8 (over z, y), head: 4 (over x, core).
Axes of the slice: x: 2, y: 2, z: 4, core: 2. Of those that a mesh axis runs over, the one named last changes fastest.
Arguments:
- queries: bfloat16 [1, 4096, 1024], P(None, 'seq', 'head'), may hold values from -40 to 40
- key_vectors: bfloat16 [1, 4096, 1024], P(None, 'seq', 'head'), may hold values from -40 to 40
- value_vectors: bfloat16 [1, 4096, 1024], P(None, 'seq', 'head'), may hold values from -6 to 6
- out_weight: bfloat16 [1024, 1024], replicated, may hold values from -0.1875 to 0.1875
Outputs:
- layer_output: bfloat16 [1, 4096, 1024], P(None, ('seq', 'head'))
All inputs are finite; a program needn't handle non-finite values.
Results may differ from a plain program's by a relative error of at most 0.038.
Values may be sent and summed in bfloat16 or wider, within the bound.
No kernel may reach another device: no remote copies, remote signals or barrier semaphores. Data moves between devices by JAX's collectives and lax.ppermute only.
A program may use at most 192 MiB of HBM per device.

v0:
```python
import jax
import jax.numpy as jnp
from jax import lax
from jax.sharding import PartitionSpec as P

HD = 64
BLOCK = 128
LEVELS = 4


neg_fill = -1e30
root_half = 0.7071067811865476


def swapped(block, axis, bit):
    count = lax.axis_size(axis)
    route = []
    for low in range(count):
        high = low | 1 << bit
        if high != low and high < count:
            route += [(low, high), (high, low)]
    return lax.ppermute(block, axis, route)


def extended(cells, sides, width):
    for axis, dim in sides:
        count = lax.axis_size(axis)
        ends = count - 1
        head = lax.slice_in_dim(cells, 0, width, axis=dim)
        tail = lax.slice_in_dim(cells, cells.shape[dim] - width, cells.shape[dim], axis=dim)
        cells = jnp.concatenate(
            [
                lax.ppermute(tail, axis, [(i, (i + 1) % count) for i in range(ends)]),
                cells,
                lax.ppermute(head, axis, [((i + 1) % count, i) for i in range(ends)]),
            ],
            axis=dim,
        )
    return cells


def pooled(field):
    shape = field.shape
    pairs = field.astype(jnp.float32).reshape(shape[:-2] + (shape[-2] // 2, 2, shape[-1]))
    return ((pairs[..., 0, :] + pairs[..., 1, :]) * root_half).astype(jnp.bfloat16)


def heads_first(field):
    samples, shard_rows, features = field.shape
    return jnp.transpose(field.reshape(samples, shard_rows, features // HD, HD), (0, 2, 1, 3))


def attend(query_blocks, key_blocks, value_blocks):
    samples, heads_here, blocks, query_count, depth = query_blocks.shape
    scaling = HD ** (-0.5)
    scores = (
        jnp.einsum(
            "shnqd,shnkd->shnqk", query_blocks, key_blocks, preferred_element_type=jnp.float32
        )
        * scaling
    )
    row_max = jnp.max(scores, axis=-1)
    chances = jnp.exp(scores - row_max[..., None]).astype(jnp.bfloat16)
    row_sum = jnp.sum(chances, axis=-1, dtype=jnp.float32)
    numerator = jnp.einsum(
        "shnqk,shnkd->shnqd", chances, value_blocks, preferred_element_type=jnp.float32
    )
    return (
        row_max.reshape(samples, heads_here, blocks * query_count),
        numerator.reshape(samples, heads_here, blocks * query_count, depth),
        row_sum.reshape(samples, heads_here, blocks * query_count),
    )


def combined(terms):
    expanded = [jnp.repeat(record[1], 2 ** record[0], axis=2) for record in terms]
    top_max = expanded[0]
    for other_max in expanded[1:]:
        top_max = jnp.maximum(top_max, other_max)
    numerator = jnp.zeros(terms[0][2].shape, jnp.float32)
    denominator = jnp.zeros(top_max.shape, jnp.float32)
    for record, fine_max in zip(terms, expanded):
        factor = jnp.exp(fine_max - top_max)
        numerator = numerator + jnp.repeat(record[2], 2 ** record[0], axis=2) * factor[..., None]
        denominator = denominator + jnp.repeat(record[3], 2 ** record[0], axis=2) * factor
    return (numerator / denominator[..., None]).astype(jnp.bfloat16)


def fetch_sibling(piece, spread, position):
    top_bit = spread.bit_length() - 1
    current = swapped(piece, "seq", top_bit)
    for low_bit in range(top_bit):
        partner_piece = swapped(current, "seq", low_bit)
        high_half = position // 2**low_bit % 2
        current = jnp.where(
            high_half == 0,
            jnp.concatenate([current, partner_piece], axis=3),
            jnp.concatenate([partner_piece, current], axis=3),
        )
    return current[:, :, :, None]


def per_device(queries, key_vectors, value_vectors, out_weight):
    samples, shard_rows, features = queries.shape
    block_rows = BLOCK
    position = lax.axis_index("seq")
    devices_seq = lax.axis_size("seq")
    blocks = shard_rows // block_rows
    heads_here = features // HD
    scaling = HD ** (-0.5)
    query_heads = heads_first(queries)
    level_kv = jnp.stack([heads_first(key_vectors), heads_first(value_vectors)])
    padded = extended(level_kv, (("seq", 3),), block_rows)

    def view(offset):
        return padded[:, :, :, offset : offset + shard_rows].reshape(
            2, samples, heads_here, blocks, block_rows, HD
        )

    sides = [view(0), view(block_rows), view(2 * block_rows)]
    query_blocks = query_heads.reshape(samples, heads_here, blocks, block_rows, HD)
    scores = (
        jnp.concatenate(
            [
                jnp.einsum(
                    "shnqd,shnkd->shnqk", query_blocks, side[0], preferred_element_type=jnp.float32
                )
                for side in sides
            ],
            axis=-1,
        )
        * scaling
    )
    global_ids = position * blocks + jnp.arange(blocks)
    left_ok = jnp.broadcast_to((global_ids > 0)[:, None], (blocks, block_rows))
    right_ok = jnp.broadcast_to(
        (global_ids < devices_seq * blocks - 1)[:, None], (blocks, block_rows)
    )
    allowed = jnp.concatenate(
        [left_ok, jnp.ones((blocks, block_rows), jnp.bool_), right_ok], axis=1
    )
    scores = jnp.where(allowed[None, None, :, None, :], scores, neg_fill)
    near_max = jnp.max(scores, axis=-1)
    chances = jnp.exp(scores - near_max[..., None]).astype(jnp.bfloat16)
    near_sum = jnp.sum(chances, axis=-1, dtype=jnp.float32)
    near_numer = jnp.zeros((samples, heads_here, blocks, block_rows, HD), jnp.float32)
    for index, side in enumerate(sides):
        near_numer = near_numer + jnp.einsum(
            "shnqk,shnkd->shnqd",
            chances[..., index * block_rows : (index + 1) * block_rows],
            side[1],
            preferred_element_type=jnp.float32,
        )
    terms = [
        (
            0,
            near_max.reshape(samples, heads_here, shard_rows),
            near_numer.reshape(samples, heads_here, shard_rows, HD),
            near_sum.reshape(samples, heads_here, shard_rows),
        )
    ]
    level_q = query_heads
    pooled_rows = shard_rows
    for ladder in range(1, LEVELS + 1):
        level_q = pooled(level_q)
        pooled_rows = shard_rows >> ladder
        if pooled_rows >= 2 * block_rows:
            level_kv = pooled(level_kv)
            grouped = level_kv.reshape(
                2, samples, heads_here, pooled_rows // (2 * block_rows), 2, block_rows, HD
            )
            partner = grouped[:, :, :, :, ::-1].reshape(
                2, samples, heads_here, pooled_rows // block_rows, block_rows, HD
            )
            level_blocks = level_q.reshape(
                samples, heads_here, pooled_rows // block_rows, block_rows, HD
            )
        else:
            level_blocks = level_q.reshape(samples, heads_here, 1, pooled_rows, HD)
            level_kv = pooled(level_kv)
            partner = fetch_sibling(level_kv, block_rows // pooled_rows, position)
        terms.append((ladder,) + attend(level_blocks, partner[0], partner[1]))
    summit = lax.all_gather(level_kv, "seq", axis=3, tiled=True)
    top_queries = level_q.reshape(samples, heads_here, 1, pooled_rows, HD)
    terms.append((LEVELS,) + attend(top_queries, summit[0][:, :, None], summit[1][:, :, None]))
    attended = jnp.transpose(combined(terms), (0, 2, 1, 3)).reshape(samples, shard_rows, features)
    return jnp.einsum(
        "brf,fg->brg",
        lax.all_to_all(attended, "head", split_axis=1, concat_axis=2, tiled=True),
        out_weight,
        preferred_element_type=jnp.float32,
    ).astype(jnp.bfloat16)


def solution(mesh):
    return jax.shard_map(
        per_device,
        mesh=mesh,
        in_specs=(P(None, "seq", "head"), P(None, "seq", "head"), P(None, "seq", "head"), P()),
        out_specs=P(None, ("seq", "head"), None),
        check_vma=False,
    )
```

profile of v0, /device:TPU:0, one launch (start us, length us, event | category | flops | bytes accessed | tf_op | source)
XLA Modules:
  0.0 179.5 jit_solution(6336453800074744161)
XLA Ops:
  0.0 1.2 copy.286
  1.2 1.1 copy.287
  3.2 5.5 %collective-permute-start = (bf16[2,1,4,128,64]{3,4,2,1,0:T(8,128)(2,1)}, bf16[2,1,4,128,64]{3,4,2,1,0:T(8,128)(2,1)}, u32[]{:S(2)}, u32[]{:S(2)}) collective-permute-start(bf16[2,1,4,128,64]{3,4,2,1,0:T(8,128)(2,1)} %get-tuple-element.30), channel_id=1, source_target_pairs={{0,4},{4,8},{8,12},{12,16},{16,20},{20,24},{24,28},{1,5},{5,9},{9,... | collective-permute-start | bytes 393224 | tf_op jit(solution)/shard_map/ppermute | solution.py:33
  8.7 1.3 collective-permute-start.1
  11.2 2.6 %maximum_convert_fusion = f32[2,1,4,256,2,64]{5,4,3,2,1,0:T(2,128)S(1)} fusion(bf16[1,1,4,256,2,64]{5,4,3,2,1,0:T(2,128)(2,1)S(1)} %bitcast.216, bf16[1,1,4,256,2,64]{5,4,3,2,1,0:T(2,128)(2,1)} %bitcast.217), kind=kLoop, calls=%fused_computation.19 | loop fusion | flops 524288 | bytes 1572864 | tf_op jit(solution)/shard_map/convert_element_type | solution.py:44
  13.9 2.7 %fusion.52 = (f32[2,1,4,256,1,64]{5,4,3,2,1,0:T(1,128)S(1)}, bf16[2,1,4,256,1,64]{5,4,3,2,1,0:T(2,128)(2,1)}) fusion(f32[2,1,4,256,2,64]{5,4,3,2,1,0:T(2,128)S(1)} %maximum_convert_fusion), kind=kLoop, calls=%fused_computation.116 | loop fusion | flops 524288 | bytes 1835008 | tf_op jit(solution)/shard_map/convert_element_type | solution.py:44
  18.8 1.6 multiply_convert_fusion.2
  20.5 2.6 %collective-permute-start.2 = (bf16[2,1,4,128,64]{3,4,2,1,0:T(8,128)(2,1)}, bf16[2,1,4,128,64]{3,4,2,1,0:T(8,128)(2,1)}, u32[]{:S(2)}, u32[]{:S(2)}) collective-permute-start(bf16[2,1,4,128,64]{3,4,2,1,0:T(8,128)(2,1)} %bitcast.28), channel_id=1, source_target_pairs={{0,4},{4,0},{8,12},{12,8},{16,20},{20,16},{24,28},{28,24},{1,5},{5... | collective-permute-start | bytes 393224 | tf_op jit(solution)/shard_map/ppermute | solution.py:22
  23.1 1.1 copy.318
  28.9 3.2 %collective-permute-start.5 = (bf16[2,1,4,32,64]{3,4,2,1,0:T(8,128)(2,1)}, bf16[2,1,4,32,64]{3,4,2,1,0:T(8,128)(2,1)}, u32[]{:S(2)}, u32[]{:S(2)}) collective-permute-start(bf16[2,1,4,32,64]{3,4,2,1,0:T(8,128)(2,1)} %bitcast.36), channel_id=1, source_target_pairs={{0,16},{16,0},{4,20},{20,4},{8,24},{24,8},{12,28},{28,12},{1,17},{... | collective-permute-start | bytes 98312 | tf_op jit(solution)/shard_map/ppermute | solution.py:22
  34.5 1.2 copy.302
  35.7 1.8 %fusion.55 = (f32[1,4,256,1,64]{4,3,2,1,0:T(1,128)}, f32[1,4,256,1,64]{4,3,2,1,0:T(1,128)}) fusion(f32[1,4,256,2,64]{4,3,2,1,0:T(2,128)S(1)} %bitcast.204), kind=kLoop, calls=%fused_computation.118 | loop fusion | bytes 1048576 | tf_op jit(solution)/shard_map/slice | solution.py:45
  37.5 1.2 copy.358
  38.7 1.2 copy.357
  42.4 1.1 fusion.57
  44.2 1.8 %copy.359 = f32[1,4,128,1,64]{2,4,3,1,0:T(8,128)} copy(f32[1,4,128,1,64]{4,3,2,1,0:T(1,128)} %get-tuple-element.33) | data formatting | bytes 262144
  47.8 1.9 %fusion.50 = (f32[1,4,64,1,64]{4,3,2,1,0:T(1,128)S(1)}, bf16[1,4,64,1,64]{4,3,2,1,0:T(2,128)(2,1)}) fusion(f32[1,4,64,2,64]{4,3,2,1,0:T(2,128)} %bitcast.220), kind=kLoop, calls=%fused_computation.115 | loop fusion | flops 65536 | bytes 229376 | tf_op jit(solution)/shard_map/convert_element_type | solution.py:44
  50.5 31.8 %all-gather = bf16[2,1,4,256,1,64]{5,2,4,1,0,3:T(4,128)(2,1)S(1)} all-gather(bf16[2,1,4,32,1,64]{5,2,4,1,0,3:T(4,128)(2,1)S(1)} %copy.324), channel_id=2, replica_groups=mesh['seq'=8,'head'=4] {'seq'}, dimensions={3}, use_global_device_ids=true | all-gather | bytes 294912 | tf_op jit(solution)/shard_map/all_gather | solution.py:183
  83.2 1.7 copy.367
  85.0 1.7 copy.368
  86.7 2.1 %fusion.54 = (bf16[1,1,4,256,1,64]{5,4,3,2,1,0:T(2,128)(2,1)}, bf16[1,1,4,256,1,64]{5,4,3,2,1,0:T(2,128)(2,1)}) fusion(bf16[2,1,4,256,1,64]{5,4,3,2,1,0:T(2,128)(2,1)S(1)} %copy-done.2), kind=kLoop, calls=%fused_computation.117 | loop fusion | bytes 524288 | tf_op jit(solution)/shard_map/slice | solution.py:182
  88.8 1.2 copy.307
  90.1 1.2 slice.156
  91.3 1.2 copy.326
  92.5 1.2 slice.175
  93.8 1.4 convolution_bitcast_fusion.1
  95.2 1.1 fusion.61
  96.3 1.3 fusion.65
  98.4 1.1 fusion.17
  99.5 1.1 fusion.20
  101.6 1.7 reshape.1723
  104.1 1.4 broadcast_in_dim.152
  105.5 1.5 broadcast_in_dim.153
  107.7 1.5 broadcast_in_dim.133
  109.2 1.0 broadcast_in_dim.142
  110.3 2.4 %copy.339 = f32[1,4,512,64]{2,3,1,0:T(8,128)} copy(f32[1,4,512,64]{3,2,1,0:T(8,128)} %bitcast.206) | data formatting | bytes 1048576 | tf_op jit(solution)/shard_map/broadcast_in_dim | solution.py:84
  113.5 1.7 broadcast_in_dim.144
  115.2 1.6 copy.341
  116.8 1.7 broadcast_in_dim.124
  118.5 1.7 copy.311
  120.2 2.4 %broadcast_in_dim.134 = f32[4,256,2,64]{3,2,1,0:T(2,128)} broadcast(f32[4,256,64]{2,1,0:T(8,128)} %bitcast.211), dimensions={0,1,3} | broadcast | bytes 786432 | tf_op jit(solution)/shard_map/broadcast_in_dim | solution.py:84
  122.5 2.4 %copy.332 = f32[1,4,512,64]{2,3,1,0:T(8,128)} copy(f32[1,4,512,64]{3,2,1,0:T(8,128)} %bitcast.205) | data formatting | bytes 1048576 | tf_op jit(solution)/shard_map/broadcast_in_dim | solution.py:84
  124.9 1.9 %maximum_select_fusion.2 = bf16[2,1,4,64,64]{3,4,2,1,0:T(8,128)(2,1)} fusion(bf16[2,1,4,32,64]{3,4,2,1,0:T(8,128)(2,1)} %collective-permute-done.6, bf16[2,1,4,32,64]{3,4,2,1,0:T(8,128)(2,1)} %collective-permute-done.5, pred[]{:T(512)S(6)} %eq.11), kind=kLoop, calls=%fused_computation.57 | loop fusion | flops 294912 | bytes 131073 | tf_op jit(solution)/shard_map/jit(_where)/select_n | solution.py:95
  126.8 2.1 %collective-permute-start.4 = (bf16[2,1,4,64,64]{3,4,2,1,0:T(8,128)(2,1)}, bf16[2,1,4,64,64]{3,4,2,1,0:T(8,128)(2,1)}, u32[]{:S(2)}, u32[]{:S(2)}) collective-permute-start(bf16[2,1,4,64,64]{3,4,2,1,0:T(8,128)(2,1)} %collective-permute-done.3), channel_id=1, source_target_pairs={{0,4},{4,0},{8,12},{12,8},{16,20},{20,16},{24,28},{28,24},{1,5},{5... | collective-permute-start | bytes 196616 | tf_op jit(solution)/shard_map/ppermute | solution.py:22
  128.9 1.9 %fusion.16 = bf16[2,1,4,64,64]{3,4,2,1,0:T(8,128)(2,1)} fusion(bf16[2,4,32,64]{2,3,1,0:T(8,128)(2,1)} %bitcast.38, bf16[2,4,32,64]{2,3,1,0:T(8,128)(2,1)} %bitcast.37, pred[]{:T(512)S(6)} %eq.11), kind=kLoop, calls=%fused_computation.56 | loop fusion | flops 294912 | bytes 131073 | tf_op jit(solution)/shard_map/concatenate | solution.py:97
  130.8 2.1 %pad_maximum_fusion = (bf16[1,1,4,512,64]{3,4,2,1,0:T(8,128)(2,1)}, bf16[1,1,4,512,64]{3,4,2,1,0:T(8,128)(2,1)}, bf16[1,1,4,512,64]{3,4,2,1,0:T(8,128)(2,1)}, bf16[1,1,4,512,64]{3,4,2,1,0:T(8,128)(2,1)}) fusion(bf16[2,1,4,128,64]{3,4,2,1,0:T(8,128)(2,1)} %collective-permute-done.1, bf16[1,1,4,512,64]{3,4,2,1,0:T(8,128)(2,1)} %bitcast.202, ...), kind=kLoop, calls=%fused_computation.29 | loop fusion | flops 3145728 | bytes 1835008 | tf_op jit(solution)/shard_map/concatenate | solution.py:31
  132.9 1.8 reshape.1725
  134.6 1.7 reshape.1719
  136.4 1.7 reshape.1715
  138.1 1.7 reshape.1721
  139.8 1.4 convolution_bitcast_fusion.2
  141.2 1.3 convolution_bitcast_fusion
  143.1 1.7 convert_reduce_fusion
  146.0 1.1 maximum_select_fusion.3
  147.4 1.2 maximum_select_fusion
  152.4 1.1 fusion.64
  158.5 1.1 fusion.27
  159.8 1.1 copy.335
  161.1 1.1 copy.336
  162.3 1.1 copy.337
  163.5 2.3 %divide_convert_fusion = bf16[1,4,512,64]{2,3,1,0:T(8,128)(2,1)S(1)} fusion(f32[1,4,512,64]{2,3,1,0:T(8,128)} %copy.339, f32[1,4,512,64]{2,3,1,0:T(8,128)} %copy.337, f32[1,4,512,64]{2,3,1,0:T(8,128)} %copy.336, f32[1,4,512,64]{2,3,1,0:T(8,128)} %copy.335, f32[1,4,512,64]{2,3,1,0:T(8,128)} %copy.332, f32[1,4,512,64]{2,3,1,0:T(8,128)} %reshape_broadcast_in_dim_reshape.9, ...), kind=kLoop, calls=%fused_computation.25 | loop fusion | flops 1703936 | bytes 3465216 | tf_op jit(solution)/shard_map/convert_element_type | solution.py:86
  167.0 2.2 %reduce.22 = bf16[512,256]{1,0:T(8,128)(2,1)S(1)} reduce(bf16[512,1,256]{2,1,0:T(2,128)(2,1)S(1)} %bitcast.215, bf16[]{:T(256)} %broadcast.472), dimensions={1}, to_apply=%bitcast.174.reduce_sub_computation | reduce | bytes 524290
  169.2 8.6 %all_to_all.15 = bf16[4,2,16384]{2,1,0:T(2,128)(2,1)S(1)} all-to-all(bf16[4,2,16384]{2,1,0:T(2,128)(2,1)S(1)} %reshape.1756), channel_id=1, replica_groups=mesh['seq'=8,'head'=4] {'head'}, dimensions={0} | all-to-all | bytes 524288 | tf_op jit(solution)/shard_map/all_to_all | solution.py:189
  178.3 1.2 fusion.2
  (140 shorter events, 34.8 us)
Async XLA Ops:
  0.0 178.3 %copy-start = (bf16[1024,1024]{1,0:T(8,128)(2,1)S(1)}, bf16[1024,1024]{1,0:T(8,128)(2,1)}, u32[]{:S(2)}) copy-start(bf16[1024,1024]{1,0:T(8,128)(2,1)} %param.7) | copy-start | bytes 6291460
  2.3 11.5 %copy-start.1 = (bf16[1,512,256]{1,2,0:T(8,128)(2,1)}, bf16[1,512,256]{1,2,0:T(8,128)(2,1)S(1)}, u32[]{:S(2)}) copy-start(bf16[1,512,256]{1,2,0:T(8,128)(2,1)S(1)} %copy.287) | copy-start | bytes 786436
  3.2 127.6 %collective-permute-start = (bf16[2,1,4,128,64]{3,4,2,1,0:T(8,128)(2,1)}, bf16[2,1,4,128,64]{3,4,2,1,0:T(8,128)(2,1)}, u32[]{:S(2)}, u32[]{:S(2)}) collective-permute-start(bf16[2,1,4,128,64]{3,4,2,1,0:T(8,128)(2,1)} %get-tuple-element.30), channel_id=1, source_target_pairs={{0,4},{4,8},{8,12},{12,16},{16,20},{20,24},{24,28},{1,5},{5,9},{9,... | collective-permute-start | bytes 393224 | tf_op jit(solution)/shard_map/ppermute | solution.py:33
  8.7 122.1 %collective-permute-start.1 = (bf16[2,1,4,128,64]{3,4,2,1,0:T(8,128)(2,1)}, bf16[2,1,4,128,64]{3,4,2,1,0:T(8,128)(2,1)}, u32[]{:S(2)}, u32[]{:S(2)}) collective-permute-start(bf16[2,1,4,128,64]{3,4,2,1,0:T(8,128)(2,1)} %get-tuple-element.31), channel_id=1, source_target_pairs={{4,0},{8,4},{12,8},{16,12},{20,16},{24,20},{28,24},{5,1},{9,5},{13... | collective-permute-start | bytes 393224 | tf_op jit(solution)/shard_map/ppermute | solution.py:35
  20.5 131.9 %collective-permute-start.2 = (bf16[2,1,4,128,64]{3,4,2,1,0:T(8,128)(2,1)}, bf16[2,1,4,128,64]{3,4,2,1,0:T(8,128)(2,1)}, u32[]{:S(2)}, u32[]{:S(2)}) collective-permute-start(bf16[2,1,4,128,64]{3,4,2,1,0:T(8,128)(2,1)} %bitcast.28), channel_id=1, source_target_pairs={{0,4},{4,0},{8,12},{12,8},{16,20},{20,16},{24,28},{28,24},{1,5},{5... | collective-permute-start | bytes 393224 | tf_op jit(solution)/shard_map/ppermute | solution.py:22
  24.9 8.1 %copy-start.15 = (bf16[1,512,256]{2,1,0:T(8,128)(2,1)S(1)}, bf16[1,512,256]{2,1,0:T(8,128)(2,1)}, u32[]{:S(2)}) copy-start(bf16[1,512,256]{2,1,0:T(8,128)(2,1)} %param.4) | copy-start | bytes 786436
  25.7 101.1 %collective-permute-start.3 = (bf16[2,1,4,64,64]{3,4,2,1,0:T(8,128)(2,1)}, bf16[2,1,4,64,64]{3,4,2,1,0:T(8,128)(2,1)}, u32[]{:S(2)}, u32[]{:S(2)}) collective-permute-start(bf16[2,1,4,64,64]{3,4,2,1,0:T(8,128)(2,1)} %bitcast.32), channel_id=1, source_target_pairs={{0,8},{8,0},{4,12},{12,4},{16,24},{24,16},{20,28},{28,20},{1,9},{9... | collective-permute-start | bytes 196616 | tf_op jit(solution)/shard_map/ppermute | solution.py:22
  28.9 71.8 %collective-permute-start.5 = (bf16[2,1,4,32,64]{3,4,2,1,0:T(8,128)(2,1)}, bf16[2,1,4,32,64]{3,4,2,1,0:T(8,128)(2,1)}, u32[]{:S(2)}, u32[]{:S(2)}) collective-permute-start(bf16[2,1,4,32,64]{3,4,2,1,0:T(8,128)(2,1)} %bitcast.36), channel_id=1, source_target_pairs={{0,16},{16,0},{4,20},{20,4},{8,24},{24,8},{12,28},{28,12},{1,17},{... | collective-permute-start | bytes 98312 | tf_op jit(solution)/shard_map/ppermute | solution.py:22
  33.1 0.7 copy-start.4
  44.2 42.5 %copy-start.2 = (bf16[2,1,4,256,1,64]{5,4,3,2,1,0:T(2,128)(2,1)S(1)}, bf16[2,1,4,256,1,64]{5,4,3,2,1,0:T(2,128)(2,1)}, u32[]{:S(2)}) copy-start(bf16[2,1,4,256,1,64]{5,4,3,2,1,0:T(2,128)(2,1)} %get-tuple-element.17) | copy-start | bytes 786436
  88.8 6.4 %copy-start.13 = (bf16[1,4,32,1,64]{4,3,2,1,0:T(2,128)(2,1)S(1)}, bf16[1,4,32,1,64]{4,3,2,1,0:T(2,128)(2,1)}, u32[]{:S(2)}) copy-start(bf16[1,4,32,1,64]{4,3,2,1,0:T(2,128)(2,1)} %fusion.32) | copy-start | bytes 49156
  93.8 5.7 %copy-start.9 = (bf16[1,1,4,1,2,128,64]{5,4,6,2,3,1,0:T(2,128)(2,1)S(1)}, bf16[1,1,4,1,2,128,64]{5,4,6,2,3,1,0:T(2,128)(2,1)}, u32[]{:S(2)}) copy-start(bf16[1,1,4,1,2,128,64]{5,4,6,2,3,1,0:T(2,128)(2,1)} %slice.175) | copy-start | bytes 393220
  98.4 44.1 %copy-start.26 = (pred[4,384]{1,0:T(4,128)(4,1)}, pred[4,384]{1,0:T(4,128)(4,1)S(1)}, u32[]{:S(2)}) copy-start(pred[4,384]{1,0:T(4,128)(4,1)S(1)} %pad_add_fusion) | copy-start | bytes 4612
  100.7 24.2 %collective-permute-start.6 = (bf16[2,1,4,32,64]{3,4,2,1,0:T(8,128)(2,1)}, bf16[2,1,4,32,64]{3,4,2,1,0:T(8,128)(2,1)}, u32[]{:S(2)}, u32[]{:S(2)}) collective-permute-start(bf16[2,1,4,32,64]{3,4,2,1,0:T(8,128)(2,1)} %collective-permute-done.5), channel_id=1, source_target_pairs={{0,4},{4,0},{8,12},{12,8},{16,20},{20,16},{24,28},{28,24},{1,5},{5... | collective-permute-start | bytes 98312 | tf_op jit(solution)/shard_map/ppermute | solution.py:22
  126.8 19.2 %collective-permute-start.7 = (bf16[2,1,4,64,64]{3,4,2,1,0:T(8,128)(2,1)}, bf16[2,1,4,64,64]{3,4,2,1,0:T(8,128)(2,1)}, u32[]{:S(2)}, u32[]{:S(2)}) collective-permute-start(bf16[2,1,4,64,64]{3,4,2,1,0:T(8,128)(2,1)} %maximum_select_fusion.2), channel_id=1, source_target_pairs={{0,8},{8,0},{4,12},{12,4},{16,24},{24,16},{20,28},{28,20},{1,9},{9... | collective-permute-start | bytes 196616 | tf_op jit(solution)/shard_map/ppermute | solution.py:22
  126.8 20.6 %collective-permute-start.4 = (bf16[2,1,4,64,64]{3,4,2,1,0:T(8,128)(2,1)}, bf16[2,1,4,64,64]{3,4,2,1,0:T(8,128)(2,1)}, u32[]{:S(2)}, u32[]{:S(2)}) collective-permute-start(bf16[2,1,4,64,64]{3,4,2,1,0:T(8,128)(2,1)} %collective-permute-done.3), channel_id=1, source_target_pairs={{0,4},{4,0},{8,12},{12,8},{16,20},{20,16},{24,28},{28,24},{1,5},{5... | collective-permute-start | bytes 196616 | tf_op jit(solution)/shard_map/ppermute | solution.py:22
  132.9 8.3 %copy-start.3 = (bf16[4,4,128,64]{2,1,3,0:T(4,128)(2,1)S(1)}, bf16[4,4,128,64]{2,1,3,0:T(4,128)(2,1)}, u32[]{:S(2)}) copy-start(bf16[4,4,128,64]{2,1,3,0:T(4,128)(2,1)} %reshape.1717) | copy-start | bytes 786436
  143.0 1.7 copy-start.5
  143.1 2.0 %copy-start.7 = (bf16[4,4,128,64]{2,1,3,0:T(4,128)(2,1)S(1)}, bf16[4,4,128,64]{2,1,3,0:T(4,128)(2,1)}, u32[]{:S(2)}) copy-start(bf16[4,4,128,64]{2,1,3,0:T(4,128)(2,1)} %reshape.1721) | copy-start | bytes 786436
  144.8 1.0 copy-start.6
  145.1 0.9 copy-start.10
  145.1 2.1 %copy-start.14 = (bf16[1,4,32,1,64]{4,3,2,1,0:T(2,128)(2,1)S(1)}, bf16[1,4,32,1,64]{4,3,2,1,0:T(2,128)(2,1)}, u32[]{:S(2)}) copy-start(bf16[1,4,32,1,64]{4,3,2,1,0:T(2,128)(2,1)} %fusion.32) | copy-start | bytes 49156
  145.1 3.6 %copy-start.11 = (bf16[1,4,64,1,64]{4,3,2,1,0:T(2,128)(2,1)S(1)}, bf16[1,4,64,1,64]{4,3,2,1,0:T(2,128)(2,1)}, u32[]{:S(2)}) copy-start(bf16[1,4,64,1,64]{4,3,2,1,0:T(2,128)(2,1)} %get-tuple-element.15) | copy-start | bytes 98308
  155.4 5.5 %copy-start.8 = (f32[4,64,64]{2,1,0:T(8,128)S(1)}, f32[4,64,64]{2,1,0:T(8,128)}, u32[]{:S(2)}) copy-start(f32[4,64,64]{2,1,0:T(8,128)} %fusion.26) | copy-start | bytes 196612
  159.8 2.4 %copy-start.12 = (f32[4,32,64]{2,1,0:T(8,128)S(1)}, f32[4,32,64]{2,1,0:T(8,128)}, u32[]{:S(2)}) copy-start(f32[4,32,64]{2,1,0:T(8,128)} %fusion.25) | copy-start | bytes 98308
  161.0 2.4 %copy-start.16 = (f32[4,512]{1,0:T(4,128)S(1)}, f32[4,512]{1,0:T(4,128)}, u32[]{:S(2)}) copy-start(f32[4,512]{1,0:T(4,128)} %broadcast_in_dim.153) | copy-start | bytes 24580
  161.0 2.4 %copy-start.17 = (f32[4,512]{1,0:T(4,128)S(1)}, f32[4,512]{1,0:T(4,128)}, u32[]{:S(2)}) copy-start(f32[4,512]{1,0:T(4,128)} %broadcast_in_dim.133) | copy-start | bytes 24580
  161.0 2.4 %copy-start.18 = (f32[4,512]{1,0:T(4,128)S(1)}, f32[4,512]{1,0:T(4,128)}, u32[]{:S(2)}) copy-start(f32[4,512]{1,0:T(4,128)} %copy.341) | copy-start | bytes 24580
  161.0 2.4 %copy-start.19 = (f32[4,512]{1,0:T(4,128)S(1)}, f32[4,512]{1,0:T(4,128)}, u32[]{:S(2)}) copy-start(f32[4,512]{1,0:T(4,128)} %copy.311) | copy-start | bytes 24580
  161.0 2.4 %copy-start.20 = (f32[4,512]{1,0:T(4,128)S(1)}, f32[4,512]{1,0:T(4,128)}, u32[]{:S(2)}) copy-start(f32[4,512]{1,0:T(4,128)} %broadcast_in_dim.127) | copy-start | bytes 24580
  161.0 2.4 %copy-start.21 = (f32[4,512]{1,0:T(4,128)S(1)}, f32[4,512]{1,0:T(4,128)}, u32[]{:S(2)}) copy-start(f32[4,512]{1,0:T(4,128)} %broadcast_in_dim.147) | copy-start | bytes 24580
  161.0 2.4 %copy-start.22 = (f32[4,512]{1,0:T(4,128)S(1)}, f32[4,512]{1,0:T(4,128)}, u32[]{:S(2)}) copy-start(f32[4,512]{1,0:T(4,128)} %broadcast_in_dim.129) | copy-start | bytes 24580
  161.0 2.4 %copy-start.23 = (f32[4,512]{1,0:T(4,128)S(1)}, f32[4,512]{1,0:T(4,128)}, u32[]{:S(2)}) copy-start(f32[4,512]{1,0:T(4,128)} %broadcast_in_dim.149) | copy-start | bytes 24580
  161.0 2.4 %copy-start.24 = (f32[4,512]{1,0:T(4,128)S(1)}, f32[4,512]{1,0:T(4,128)}, u32[]{:S(2)}) copy-start(f32[4,512]{1,0:T(4,128)} %broadcast_in_dim.131) | copy-start | bytes 24580
  161.1 2.4 %copy-start.25 = (f32[4,512]{1,0:T(4,128)S(1)}, f32[4,512]{1,0:T(4,128)}, u32[]{:S(2)}) copy-start(f32[4,512]{1,0:T(4,128)} %broadcast_in_dim.151) | copy-start | bytes 24580
where the time goes:
time: 181 us; the launch traced here: 180 us
  local copies, waits for them, and re-layouts  77.9 us (43%)
  blocking collectives  40.4 us (22%)
  other arithmetic  29.6 us (16%)
  starting transfers between devices  15.8 us (9%)
  matrix products  15 us (8%)
    all_gather x1, blocking collectives, per_device(): summit = lax.all_gather(level_kv, 'seq', axis=3, tiled=True)  31.8 us
    unnamed x73, local copies, waits for them, and re-layouts  14.7 us
    broadcast_in_dim x10, local copies, waits for them, and re-layouts, combined(): jnp.repeat(record[2], 2 ** record[0], axis=2) * factor[..., None]  11.9 us
    another operation x7, local copies, waits for them, and re-layouts  10.2 us
    ppermute x6, starting transfers between devices, swapped(): return lax.ppermute(block, axis, route)  8.97 us
    broadcast_in_dim x10, local copies, waits for them, and re-layouts, combined(): jnp.repeat(record[3], 2 ** record[0], axis=2) * factor  8.72 us
    all_to_all x1, blocking collectives, per_device(): lax.all_to_all(attended, 'head', split_axis=1, concat_axis=2, tiled=True)  8.6 us
    broadcast_in_dim x10, local copies, waits for them, and re-layouts, combined(): jnp.repeat(record[1], 2 ** record[0], axis=2)  8.05 us
  transfers between devices with their start and end apart: 8, of which 0 were waited for; matrix products, arithmetic and copies ran while one was open for 56% of the time, Pallas kernels for 0%

commit v1 on v0

v1 whole, which is shorter than its diff:
```python
import jax
import jax.numpy as jnp
from jax import lax
from jax.experimental import pallas as pl
from jax.experimental.pallas import tpu as pltpu
from jax.sharding import PartitionSpec as P

HD = 64
BLOCK = 128
LEVELS = 4
SLAB = 8
PAIR = 2 * HD

neg_fill = -1e30
root_half = 0.7071067811865476
log2_scale = HD**-0.5 * 1.4426950408889634

FAN = 2**LEVELS


def slabs_of(scratch, block):
    return [scratch[pl.ds(BLOCK * block + j, SLAB, stride=FAN), :] for j in range(FAN)]


def pooled_slabs(slabs):
    return [
        ((low + high) * root_half).astype(jnp.bfloat16).astype(jnp.float32)
        for low, high in zip(slabs[0::2], slabs[1::2])
    ]


def joined(slabs):
    return jnp.concatenate(slabs, axis=0).astype(jnp.bfloat16)


def spill(source, scratch):
    for half in range(scratch.shape[0]):
        scratch[half] = source[:, half * PAIR : (half + 1) * PAIR].astype(jnp.float32)


def pool_kernel(k_ref, v_ref, first_ref, second_ref, one_ref, three_ref, four_ref, scratch):
    rows = k_ref.shape[0]
    blocks = rows // BLOCK
    even = lax.rem(lax.axis_index("seq"), 2) == 0
    for which, ref in enumerate((k_ref, v_ref)):
        head, tail = ref[:BLOCK, :], ref[rows - BLOCK :, :]
        first_ref[2 + which] = jnp.where(even, tail, head)
        second_ref[which] = jnp.where(even, head, tail)
        spill(ref, scratch)
        for half in range(scratch.shape[0]):
            lanes = pl.ds(half * PAIR, PAIR)
            ladder = [[], [], [], [], []]
            for block in range(blocks):
                slabs = slabs_of(scratch.at[half], block)
                for level in range(1, LEVELS + 1):
                    slabs = pooled_slabs(slabs)
                    ladder[level] += slabs
            one_ref[which, :, lanes] = joined(ladder[1])
            first_ref[which, :, lanes] = joined(ladder[2])
            three_ref[which, :, lanes] = joined(ladder[3])
            four_ref[which, :, lanes] = joined(ladder[4])


def term(queries, keys, values, left_open=None, right_open=None):
    rows = queries.shape[0]
    low = lax.broadcasted_iota(jnp.int32, (rows, PAIR), 1) < HD
    zero = jnp.zeros_like(queries)
    both = jnp.concatenate([jnp.where(low, queries, zero), jnp.where(low, zero, queries)], axis=0)
    scores = log2_scale * lax.dot_general(
        both, keys, (((1,), (1,)), ((), ())), preferred_element_type=jnp.float32
    )
    if left_open is not None:
        parts = [scores[:, :BLOCK], scores[:, BLOCK : 2 * BLOCK], scores[:, 2 * BLOCK :]]
        parts[0] = jnp.where(left_open, parts[0], neg_fill)
        parts[2] = jnp.where(right_open, parts[2], neg_fill)
        scores = jnp.concatenate(parts, axis=1)
    top = jnp.max(scores, axis=1, keepdims=True)
    weights = jnp.exp2(scores - top).astype(jnp.bfloat16)
    result = jnp.dot(weights, values, preferred_element_type=jnp.float32)
    return (
        jnp.where(low, top[:rows], top[rows:]),
        jnp.where(low, result[:rows, :PAIR], result[rows:, :PAIR]),
        jnp.where(low, result[:rows, PAIR:], result[rows:, PAIR:]),
    )


def merged(fine, coarse):
    top = jnp.maximum(fine[0], coarse[0])
    keep = jnp.exp2(fine[0] - top)
    join = jnp.exp2(coarse[0] - top)
    return top, fine[1] * keep + coarse[1] * join, fine[2] * keep + coarse[2] * join


def doubled(field):
    rows, lanes = field.shape
    slabs = field.reshape(rows // SLAB, 1, SLAB, lanes)
    return jnp.broadcast_to(slabs, (rows // SLAB, 2, SLAB, lanes)).reshape(2 * rows, lanes)


def with_ones(values, weight=1.0):
    if weight != 1.0:
        values = values * jnp.bfloat16(weight)
    return jnp.concatenate([values, jnp.full(values.shape, weight, jnp.bfloat16)], axis=1)


def attend_kernel(
    q_ref, k_ref, v_ref, one_ref, first_ref, second_ref, three_a, three_b, four_ref, rest_ref,
    *tail,
):
    outs, (scratch, fine_q, padded, state) = tail[:-4], tail[-4:]
    rows = q_ref.shape[0]
    blocks = rows // BLOCK
    position = lax.axis_index("seq")
    even = lax.rem(position, 2) == 0
    left_open = position > 0
    right_open = position < lax.axis_size("seq") - 1
    own = lax.axis_index("head")

    for which, ref in enumerate((k_ref, v_ref)):
        inner, outer = first_ref[2 + which], second_ref[which]
        padded[which, :BLOCK, :] = jnp.where(even, outer, inner)
        padded[which, BLOCK : BLOCK + rows, :] = ref[...]
        padded[which, BLOCK + rows :, :] = jnp.where(even, inner, outer)

    spill(q_ref, scratch)
    pairs = scratch.shape[0]
    for pair in range(pairs):
        lanes = pl.ds(pair * PAIR, PAIR)
        ladder = [[], [], [], [], []]
        for block in range(blocks):
            slabs = slabs_of(scratch.at[pair], block)
            ladder[0] += slabs
            for level in range(1, LEVELS + 1):
                slabs = pooled_slabs(slabs)
                ladder[level] += slabs
        fine_q[:, lanes] = joined(ladder[0])
        coarse_q = [None] + [joined(ladder[level]) for level in range(1, LEVELS + 1)]

        sibling = 4 * (rows >> LEVELS)
        ours, others = four_ref[:, :, lanes], rest_ref[:, :, lanes]
        keys = jnp.concatenate([ours[0], others[0]], axis=0)
        values = jnp.concatenate(
            [with_ones(ours[1]), with_ones(others[1, :sibling], 2.0)]
            + ([with_ones(others[1, sibling:])] if others.shape[1] > sibling else []),
            axis=0,
        )
        now = term(coarse_q[4], keys, values)
        keys = jnp.concatenate([three_a[0, :, lanes], three_b[0, :, lanes]], axis=0)
        values = jnp.concatenate([three_a[1, :, lanes], three_b[1, :, lanes]], axis=0)
        now = merged(term(coarse_q[3], keys, with_ones(values)), [doubled(x) for x in now])
        now = merged(
            term(coarse_q[2], first_ref[0, :, lanes], with_ones(first_ref[1, :, lanes])),
            [doubled(x) for x in now],
        )
        up = [doubled(x) for x in now]
        for half in range(2):
            there = pl.ds((1 - half) * BLOCK, BLOCK)
            here = slice(half * BLOCK, (half + 1) * BLOCK)
            done = merged(
                term(coarse_q[1][here], one_ref[0, there, lanes], with_ones(one_ref[1, there, lanes])),
                [x[here] for x in up],
            )
            for index, field in enumerate(done):
                state[index, here, lanes] = field

    for step, out in enumerate(outs):
        block = own ^ step
        start = pl.multiple_of(block * BLOCK, BLOCK)
        half_start = pl.multiple_of(block * (BLOCK // 2), BLOCK // 2)
        left = jnp.logical_or(left_open, block > 0)
        right = jnp.logical_or(right_open, block < blocks - 1)
        for pair in range(pairs):
            lanes = pl.ds(pair * PAIR, PAIR)
            near = term(
                fine_q[pl.ds(start, BLOCK), lanes],
                padded[0, pl.ds(start, 3 * BLOCK), lanes],
                with_ones(padded[1, pl.ds(start, 3 * BLOCK), lanes]),
                left,
                right,
            )
            coarse = [doubled(state[index, pl.ds(half_start, BLOCK // 2), lanes]) for index in range(3)]
            _, numer, rowsum = merged(near, coarse)
            out[:, lanes] = (numer / rowsum).astype(jnp.bfloat16)


def project_kernel(*refs):
    parts, (weight_ref, out_ref, scratch) = refs[:-3], refs[-3:]
    own = lax.axis_index("head")
    total = None
    for step, part in enumerate(parts):
        start = pl.multiple_of((own ^ step) * part.shape[1], part.shape[1])
        product = jnp.dot(
            part[...], weight_ref[pl.ds(start, part.shape[1]), :], preferred_element_type=jnp.float32
        )
        total = product if total is None else total + product
    count = scratch.shape[0]
    for column in range(count):
        scratch[column] = total[:, column * PAIR : (column + 1) * PAIR]
    for column in range(count):
        for i in range(SLAB):
            out_ref[i * FAN : (i + 1) * FAN, column * PAIR : (column + 1) * PAIR] = scratch[
                column, pl.ds(i, FAN, stride=SLAB), :
            ].astype(jnp.bfloat16)


def swapped(block, axis, mask):
    return lax.ppermute(block, axis, [(i, i ^ mask) for i in range(lax.axis_size(axis))])


def across(block, axis):
    count = lax.axis_size(axis)
    route = []
    for low in range(1, count - 1, 2):
        route += [(low, low + 1), (low + 1, low)]
    return lax.ppermute(block, axis, route)


def per_device(queries, key_vectors, value_vectors, out_weight):
    rows, features = queries.shape[1:]
    queries, key_vectors, value_vectors = queries[0], key_vectors[0], value_vectors[0]
    pairs = features // PAIR
    seq_count, head_count = lax.axis_size("seq"), lax.axis_size("head")
    bf16 = lambda *shape: jax.ShapeDtypeStruct(shape, jnp.bfloat16)
    params = pltpu.CompilerParams(vmem_limit_bytes=32 * 1024 * 1024)

    first, second, one, three, four = pl.pallas_call(
        pool_kernel,
        out_shape=[
            bf16(4, BLOCK, features),
            bf16(2, BLOCK, features),
            bf16(2, rows // 2, features),
            bf16(2, rows // 8, features),
            bf16(2, rows // 16, features),
        ],
        scratch_shapes=[pltpu.VMEM((pairs, rows, PAIR), jnp.float32)],
        compiler_params=params,
        name="pool",
    )(key_vectors, value_vectors)

    first = swapped(first, "seq", 1)
    second = across(second, "seq")
    three_a, three_b = swapped(three, "seq", 2), swapped(three, "seq", 3)
    fours = [swapped(four, "seq", mask) for mask in range(1, 8)]
    ours = jnp.concatenate([four] + fours[:3], axis=1)
    rest = jnp.concatenate(fours[3:], axis=1)
    group = 8
    while group < seq_count:
        known = jnp.concatenate([ours, rest], axis=1)
        rest = jnp.concatenate([rest, swapped(known, "seq", group)], axis=1)
        group *= 2

    outs = pl.pallas_call(
        attend_kernel,
        out_shape=[bf16(BLOCK, features) for _ in range(head_count)],
        scratch_shapes=[
            pltpu.VMEM((pairs, rows, PAIR), jnp.float32),
            pltpu.VMEM((rows, features), jnp.bfloat16),
            pltpu.VMEM((2, rows + 2 * BLOCK, features), jnp.bfloat16),
            pltpu.VMEM((3, rows // 2, features), jnp.float32),
        ],
        compiler_params=params,
        name="attend",
    )(queries, key_vectors, value_vectors, one, first, second, three_a, three_b, ours, rest)

    parts = [part if step == 0 else swapped(part, "head", step) for step, part in enumerate(outs)]
    width = out_weight.shape[1]
    result = pl.pallas_call(
        project_kernel,
        out_shape=bf16(BLOCK, width),
        scratch_shapes=[pltpu.VMEM((width // PAIR, BLOCK, PAIR), jnp.float32)],
        compiler_params=params,
        name="project",
    )(*parts, out_weight)
    return result[None]


def solution(mesh):
    return jax.shard_map(
        per_device,
        mesh=mesh,
        in_specs=(P(None, "seq", "head"), P(None, "seq", "head"), P(None, "seq", "head"), P()),
        out_specs=P(None, ("seq", "head"), None),
        check_vma=False,
    )
```

time: 181 us -> 37.2 us (0.21)
  local copies, waits for them, and re-layouts: 77.9 us -> 3 us
  blocking collectives: 40.4 us -> 0 us
  other arithmetic: 29.6 us -> 0.02 us
  matrix products: 15 us -> 0 us
  waiting for transfers between devices: 0.02 us -> 7.62 us
  starting transfers between devices: 15.8 us -> 21.3 us
  Pallas kernels: 0 us -> 5.02 us
    all_gather x1 -> x0, blocking collectives: 31.8 us -> none  [per_device(): summit = lax.all_gather(level_kv, 'seq', axis=3, tiled=True)]
    broadcast_in_dim x33 -> x0, local copies, waits for them, and re-layouts: 29.4 us -> none  [the longest x10 11.9 us: combined(): jnp.repeat(record[2], 2 ** record[0], axis=2) * factor[..., None]]
    convert_element_type x10 -> x0, other arithmetic: 14.3 us -> none  [the longest x3 7.26 us: pooled(): field.astype(jnp.float32)]
    dot_general x16 -> x0, matrix products: 13.9 us -> none  [the longest x3 4.09 us: per_device(): jnp.einsum('shnqd,shnkd->shnqk', query_blocks, side[0], preferred_element...]
    slice x13 -> x0, local copies, waits for them, and re-layouts: 12.7 us -> none  [the longest x7 7.01 us: per_device(): terms.append((ladder,) + attend(level_blocks, partner[0], partner[1]))]
    unnamed x73 -> x8, local copies, waits for them, and re-layouts: 14.7 us -> 3 us
    another operation x8 -> x0, local copies, waits for them, and re-layouts: 11.2 us -> none
    all_to_all x1 -> x0, blocking collectives: 8.6 us -> none  [per_device(): lax.all_to_all(attended, 'head', split_axis=1, concat_axis=2, tiled=True)]
  transfers between devices with their start and end apart: 8 -> 14, of which waited for: 0 -> 5; matrix products, arithmetic and copies ran while one was open for 56% -> 0% of each run, Pallas kernels for 0% -> 0%
where the time goes in v1:
time: 37.2 us; the launch traced here: 37.1 us
  starting transfers between devices  21.3 us (57%)
  waiting for transfers between devices  7.62 us (20%)
  Pallas kernels  5.02 us (13%)
  local copies, waits for them, and re-layouts  3 us (8%)
    ppermute x13, starting transfers between devices, swapped(): lax.ppermute(block, axis, [(i, i ^ mask) for i in range(lax.axis_size(axi...  20.7 us
    ppermute x13, waiting for transfers between devices, swapped(): lax.ppermute(block, axis, [(i, i ^ mask) for i in range(lax.axis_size(axi...  7.62 us
    pallas_call x1, Pallas kernels, per_device(): pl.pallas_call(attend_kernel, out_shape=[bf16(BLOCK, features) for _ in r...  3.32 us
    unnamed x8, local copies, waits for them, and re-layouts  3 us
    pallas_call x1, Pallas kernels, per_device(): pl.pallas_call(project_kernel, out_shape=bf16(BLOCK, width), scratch_shap...  1.23 us
  transfers between devices with their start and end apart: 14, of which 5 were waited for; matrix products, arithmetic and copies ran while one was open for 0% of the time, Pallas kernels for 0%

profile of v1, /device:TPU:0, one launch (start us, length us, event | category | flops | bytes accessed | tf_op | source)
XLA Modules:
  0.0 37.1 jit_solution(7743206586703550585)
XLA Ops:
  0.0 0.0 copy-start
  0.0 0.0 copy-start.1
  0.0 1.1 %copy-done.1 = bf16[1,512,256]{2,1,0:T(8,128)(2,1)S(1)} copy-done((bf16[1,512,256]{2,1,0:T(8,128)(2,1)S(1)}, bf16[1,512,256]{2,1,0:T(8,128)(2,1)}, u32[]{:S(2)}) %copy-start.1) | copy-done | bytes 262168
  1.1 0.0 copy-start.2
  1.1 0.9 %copy-done.2 = bf16[1,512,256]{2,1,0:T(8,128)(2,1)S(1)} copy-done((bf16[1,512,256]{2,1,0:T(8,128)(2,1)S(1)}, bf16[1,512,256]{2,1,0:T(8,128)(2,1)}, u32[]{:S(2)}) %copy-start.2) | copy-done | bytes 262168
  2.1 0.5 %pool.1 = (bf16[4,128,256]{2,1,0:T(8,128)(2,1)S(1)}, bf16[2,128,256]{2,1,0:T(8,128)(2,1)S(1)}, bf16[2,256,256]{2,1,0:T(8,128)(2,1)S(1)}, bf16[2,64,256]{2,1,0:T(8,128)(2,1)S(1)}, bf16[2,32,256]{2,1,0:T(8,128)(2,1)S(1)}) custom-call(bf16[512,256]{1,0:T(8,128)(2,1)S(1)} %bitcast.4, bf16[512,256]{1,0:T(8,128)(2,1)S(1)} %bitcast.6), custom_call_target="tpu_custom_call" | custom-call | tf_op jit(solution)/shard_map/pool/pallas_call | solution.py:226
  2.5 4.0 %collective-permute-start.6 = (bf16[2,32,256]{2,1,0:T(8,128)(2,1)S(1)}, bf16[2,32,256]{2,1,0:T(8,128)(2,1)S(1)}, u32[]{:S(2)}, u32[]{:S(2)}) collective-permute-start(bf16[2,32,256]{2,1,0:T(8,128)(2,1)S(1)} %get-tuple-element.18), channel_id=1, source_target_pairs={{0,12},{4,8},{8,4},{12,0},{16,28},{20,24},{24,20},{28,16},{1,13},{... | collective-permute-start | bytes 98312 | tf_op jit(solution)/shard_map/ppermute | solution.py:207
  6.6 0.4 %collective-permute-start.5 = (bf16[2,32,256]{2,1,0:T(8,128)(2,1)S(1)}, bf16[2,32,256]{2,1,0:T(8,128)(2,1)S(1)}, u32[]{:S(2)}, u32[]{:S(2)}) collective-permute-start(bf16[2,32,256]{2,1,0:T(8,128)(2,1)S(1)} %get-tuple-element.18), channel_id=1, source_target_pairs={{0,8},{4,12},{8,0},{12,4},{16,24},{20,28},{24,16},{28,20},{1,9},{5... | collective-permute-start | bytes 98312 | tf_op jit(solution)/shard_map/ppermute | solution.py:207
  7.0 0.2 collective-permute-start.4
  7.2 4.9 %collective-permute-start.10 = (bf16[2,32,256]{2,1,0:T(8,128)(2,1)S(1)}, bf16[2,32,256]{2,1,0:T(8,128)(2,1)S(1)}, u32[]{:S(2)}, u32[]{:S(2)}) collective-permute-start(bf16[2,32,256]{2,1,0:T(8,128)(2,1)S(1)} %get-tuple-element.18), channel_id=1, source_target_pairs={{0,28},{4,24},{8,20},{12,16},{16,12},{20,8},{24,4},{28,0},{1,29},{... | collective-permute-start | bytes 98312 | tf_op jit(solution)/shard_map/ppermute | solution.py:207
  12.1 0.5 %collective-permute-start = (bf16[4,128,256]{2,1,0:T(8,128)(2,1)S(1)}, bf16[4,128,256]{2,1,0:T(8,128)(2,1)S(1)}, u32[]{:S(2)}, u32[]{:S(2)}) collective-permute-start(bf16[4,128,256]{2,1,0:T(8,128)(2,1)S(1)} %get-tuple-element.15), channel_id=1, source_target_pairs={{0,4},{4,0},{8,12},{12,8},{16,20},{20,16},{24,28},{28,24},{1,5},{5... | collective-permute-start | bytes 786440 | tf_op jit(solution)/shard_map/ppermute | solution.py:207
  12.6 0.0 collective-permute-done.6
  12.6 0.1 collective-permute-start.9
  12.7 0.0 collective-permute-done.5
  12.7 1.9 %collective-permute-start.8 = (bf16[2,32,256]{2,1,0:T(8,128)(2,1)S(1)}, bf16[2,32,256]{2,1,0:T(8,128)(2,1)S(1)}, u32[]{:S(2)}, u32[]{:S(2)}) collective-permute-start(bf16[2,32,256]{2,1,0:T(8,128)(2,1)S(1)} %get-tuple-element.18), channel_id=1, source_target_pairs={{0,20},{4,16},{8,28},{12,24},{16,4},{20,0},{24,12},{28,8},{1,21},{... | collective-permute-start | bytes 98312 | tf_op jit(solution)/shard_map/ppermute | solution.py:207
  14.6 0.0 collective-permute-done.4
  14.6 2.1 %collective-permute-start.7 = (bf16[2,32,256]{2,1,0:T(8,128)(2,1)S(1)}, bf16[2,32,256]{2,1,0:T(8,128)(2,1)S(1)}, u32[]{:S(2)}, u32[]{:S(2)}) collective-permute-start(bf16[2,32,256]{2,1,0:T(8,128)(2,1)S(1)} %get-tuple-element.18), channel_id=1, source_target_pairs={{0,16},{4,20},{8,24},{12,28},{16,0},{20,4},{24,8},{28,12},{1,17},{... | collective-permute-start | bytes 98312 | tf_op jit(solution)/shard_map/ppermute | solution.py:207
  16.7 0.0 collective-permute-done.10
  16.7 0.7 %collective-permute-start.1 = (bf16[2,128,256]{2,1,0:T(8,128)(2,1)S(1)}, bf16[2,128,256]{2,1,0:T(8,128)(2,1)S(1)}, u32[]{:S(2)}, u32[]{:S(2)}) collective-permute-start(bf16[2,128,256]{2,1,0:T(8,128)(2,1)S(1)} %get-tuple-element.16), channel_id=1, source_target_pairs={{4,8},{8,4},{12,16},{16,12},{20,24},{24,20},{5,9},{9,5},{13,17},{1... | collective-permute-start | bytes 393224 | tf_op jit(solution)/shard_map/ppermute | solution.py:215
  17.4 0.9 %collective-permute-done.9 = bf16[2,32,256]{2,1,0:T(8,128)(2,1)S(1)} collective-permute-done((bf16[2,32,256]{2,1,0:T(8,128)(2,1)S(1)}, bf16[2,32,256]{2,1,0:T(8,128)(2,1)S(1)}, u32[]{:S(2)}, u32[]{:S(2)}) %collective-permute-start.9) | collective-permute-done | bytes 32800 | tf_op jit(solution)/shard_map/ppermute | solution.py:207
  18.3 2.2 %collective-permute-start.2 = (bf16[2,64,256]{2,1,0:T(8,128)(2,1)S(1)}, bf16[2,64,256]{2,1,0:T(8,128)(2,1)S(1)}, u32[]{:S(2)}, u32[]{:S(2)}) collective-permute-start(bf16[2,64,256]{2,1,0:T(8,128)(2,1)S(1)} %get-tuple-element.17), channel_id=1, source_target_pairs={{0,8},{4,12},{8,0},{12,4},{16,24},{20,28},{24,16},{28,20},{1,9},{5... | collective-permute-start | bytes 196616 | tf_op jit(solution)/shard_map/ppermute | solution.py:207
  20.5 0.0 collective-permute-done.8
  20.5 2.4 %collective-permute-start.3 = (bf16[2,64,256]{2,1,0:T(8,128)(2,1)S(1)}, bf16[2,64,256]{2,1,0:T(8,128)(2,1)S(1)}, u32[]{:S(2)}, u32[]{:S(2)}) collective-permute-start(bf16[2,64,256]{2,1,0:T(8,128)(2,1)S(1)} %get-tuple-element.17), channel_id=1, source_target_pairs={{0,12},{4,8},{8,4},{12,0},{16,28},{20,24},{24,20},{28,16},{1,13},{... | collective-permute-start | bytes 196616 | tf_op jit(solution)/shard_map/ppermute | solution.py:207
  22.9 0.0 collective-permute-done.7
  22.9 1.5 %collective-permute-done.2.three_a = bf16[2,64,256]{2,1,0:T(8,128)(2,1)S(1)} collective-permute-done((bf16[2,64,256]{2,1,0:T(8,128)(2,1)S(1)}, bf16[2,64,256]{2,1,0:T(8,128)(2,1)S(1)}, u32[]{:S(2)}, u32[]{:S(2)}) %collective-permute-start.2) | collective-permute-done | bytes 65568 | tf_op jit(solution)/shard_map/ppermute | solution.py:207
  24.4 1.5 %collective-permute-done.3.three_b = bf16[2,64,256]{2,1,0:T(8,128)(2,1)S(1)} collective-permute-done((bf16[2,64,256]{2,1,0:T(8,128)(2,1)S(1)}, bf16[2,64,256]{2,1,0:T(8,128)(2,1)S(1)}, u32[]{:S(2)}, u32[]{:S(2)}) %collective-permute-start.3) | collective-permute-done | bytes 65568 | tf_op jit(solution)/shard_map/ppermute | solution.py:207
  25.8 0.0 collective-permute-done.1.second_ref
  25.8 0.0 collective-permute-done.first_ref
  25.8 0.0 copy-start.3
  25.8 0.9 %copy-done.3 = bf16[1,512,256]{2,1,0:T(8,128)(2,1)S(1)} copy-done((bf16[1,512,256]{2,1,0:T(8,128)(2,1)S(1)}, bf16[1,512,256]{2,1,0:T(8,128)(2,1)}, u32[]{:S(2)}) %copy-start.3) | copy-done | bytes 262168
  26.8 3.3 %attend.1 = (bf16[128,256]{1,0:T(8,128)(2,1)S(1)}, bf16[128,256]{1,0:T(8,128)(2,1)S(1)}, bf16[128,256]{1,0:T(8,128)(2,1)S(1)}, bf16[128,256]{1,0:T(8,128)(2,1)S(1)}) custom-call(bf16[512,256]{1,0:T(8,128)(2,1)S(1)} %bitcast.8, bf16[512,256]{1,0:T(8,128)(2,1)S(1)} %bitcast.5, bf16[512,256]{1,0:T(8,128)(2,1)S(1)} %bitcast.7, ...), custom_call_target="tpu_custom_call" | custom-call | tf_op jit(solution)/shard_map/attend/pallas_call | solution.py:252
  30.1 0.1 collective-permute-start.11
  30.2 1.6 %collective-permute-start.12 = (bf16[128,256]{1,0:T(8,128)(2,1)S(1)}, bf16[128,256]{1,0:T(8,128)(2,1)S(1)}, u32[]{:S(2)}, u32[]{:S(2)}) collective-permute-start(bf16[128,256]{1,0:T(8,128)(2,1)S(1)} %get-tuple-element.21), channel_id=1, source_target_pairs={{0,2},{1,3},{2,0},{3,1},{4,6},{5,7},{6,4},{7,5},{8,10},{9,11},{10,... | collective-permute-start | bytes 196616 | tf_op jit(solution)/shard_map/ppermute | solution.py:207
  31.8 0.3 collective-permute-start.13
  32.1 0.0 collective-permute-done.11.refs_1_
  32.1 2.6 %collective-permute-done.12.refs_2_ = bf16[128,256]{1,0:T(8,128)(2,1)S(1)} collective-permute-done((bf16[128,256]{1,0:T(8,128)(2,1)S(1)}, bf16[128,256]{1,0:T(8,128)(2,1)S(1)}, u32[]{:S(2)}, u32[]{:S(2)}) %collective-permute-start.12) | collective-permute-done | bytes 65568 | tf_op jit(solution)/shard_map/ppermute | solution.py:207
  34.7 1.1 %collective-permute-done.13.refs_3_ = bf16[128,256]{1,0:T(8,128)(2,1)S(1)} collective-permute-done((bf16[128,256]{1,0:T(8,128)(2,1)S(1)}, bf16[128,256]{1,0:T(8,128)(2,1)S(1)}, u32[]{:S(2)}, u32[]{:S(2)}) %collective-permute-start.13) | collective-permute-done | bytes 65568 | tf_op jit(solution)/shard_map/ppermute | solution.py:207
  35.8 0.0 copy-done
  35.8 1.2 %project.1 = bf16[128,1024]{1,0:T(8,128)(2,1)} custom-call(bf16[128,256]{1,0:T(8,128)(2,1)S(1)} %get-tuple-element.19.refs_0_, bf16[128,256]{1,0:T(8,128)(2,1)S(1)} %collective-permute-done.11.refs_1_, bf16[128,256]{1,0:T(8,128)(2,1)S(1)} %collective-permute-done.12.refs_2_, bf16[128,256]{1,0:T(8,128)(2,1)S(1)} %collective-permute-done.13.refs_3_, ...), custom_call_target="tpu_custom_call" | custom-call | tf_op jit(solution)/shard_map/project/pallas_call | solution.py:267
  (2 shorter events, 0.0 us)
Async XLA Ops:
  0.0 35.8 %copy-start = (bf16[1024,1024]{1,0:T(8,128)(2,1)S(1)}, bf16[1024,1024]{1,0:T(8,128)(2,1)}, u32[]{:S(2)}) copy-start(bf16[1024,1024]{1,0:T(8,128)(2,1)} %refs_4_.1) | copy-start | bytes 6291460
  0.0 1.1 %copy-start.1 = (bf16[1,512,256]{2,1,0:T(8,128)(2,1)S(1)}, bf16[1,512,256]{2,1,0:T(8,128)(2,1)}, u32[]{:S(2)}) copy-start(bf16[1,512,256]{2,1,0:T(8,128)(2,1)} %param.5) | copy-start | bytes 786436
  1.1 0.9 %copy-start.2 = (bf16[1,512,256]{2,1,0:T(8,128)(2,1)S(1)}, bf16[1,512,256]{2,1,0:T(8,128)(2,1)}, u32[]{:S(2)}) copy-start(bf16[1,512,256]{2,1,0:T(8,128)(2,1)} %param.6) | copy-start | bytes 786436
  2.5 10.1 %collective-permute-start.6 = (bf16[2,32,256]{2,1,0:T(8,128)(2,1)S(1)}, bf16[2,32,256]{2,1,0:T(8,128)(2,1)S(1)}, u32[]{:S(2)}, u32[]{:S(2)}) collective-permute-start(bf16[2,32,256]{2,1,0:T(8,128)(2,1)S(1)} %get-tuple-element.18), channel_id=1, source_target_pairs={{0,12},{4,8},{8,4},{12,0},{16,28},{20,24},{24,20},{28,16},{1,13},{... | collective-permute-start | bytes 98312 | tf_op jit(solution)/shard_map/ppermute | solution.py:207
  6.6 6.1 %collective-permute-start.5 = (bf16[2,32,256]{2,1,0:T(8,128)(2,1)S(1)}, bf16[2,32,256]{2,1,0:T(8,128)(2,1)S(1)}, u32[]{:S(2)}, u32[]{:S(2)}) collective-permute-start(bf16[2,32,256]{2,1,0:T(8,128)(2,1)S(1)} %get-tuple-element.18), channel_id=1, source_target_pairs={{0,8},{4,12},{8,0},{12,4},{16,24},{20,28},{24,16},{28,20},{1,9},{5... | collective-permute-start | bytes 98312 | tf_op jit(solution)/shard_map/ppermute | solution.py:207
  7.0 7.6 %collective-permute-start.4 = (bf16[2,32,256]{2,1,0:T(8,128)(2,1)S(1)}, bf16[2,32,256]{2,1,0:T(8,128)(2,1)S(1)}, u32[]{:S(2)}, u32[]{:S(2)}) collective-permute-start(bf16[2,32,256]{2,1,0:T(8,128)(2,1)S(1)} %get-tuple-element.18), channel_id=1, source_target_pairs={{0,4},{4,0},{8,12},{12,8},{16,20},{20,16},{24,28},{28,24},{1,5},{5... | collective-permute-start | bytes 98312 | tf_op jit(solution)/shard_map/ppermute | solution.py:207
  7.2 9.5 %collective-permute-start.10 = (bf16[2,32,256]{2,1,0:T(8,128)(2,1)S(1)}, bf16[2,32,256]{2,1,0:T(8,128)(2,1)S(1)}, u32[]{:S(2)}, u32[]{:S(2)}) collective-permute-start(bf16[2,32,256]{2,1,0:T(8,128)(2,1)S(1)} %get-tuple-element.18), channel_id=1, source_target_pairs={{0,28},{4,24},{8,20},{12,16},{16,12},{20,8},{24,4},{28,0},{1,29},{... | collective-permute-start | bytes 98312 | tf_op jit(solution)/shard_map/ppermute | solution.py:207
  12.1 13.8 %collective-permute-start = (bf16[4,128,256]{2,1,0:T(8,128)(2,1)S(1)}, bf16[4,128,256]{2,1,0:T(8,128)(2,1)S(1)}, u32[]{:S(2)}, u32[]{:S(2)}) collective-permute-start(bf16[4,128,256]{2,1,0:T(8,128)(2,1)S(1)} %get-tuple-element.15), channel_id=1, source_target_pairs={{0,4},{4,0},{8,12},{12,8},{16,20},{20,16},{24,28},{28,24},{1,5},{5... | collective-permute-start | bytes 786440 | tf_op jit(solution)/shard_map/ppermute | solution.py:207
  12.6 5.7 %collective-permute-start.9 = (bf16[2,32,256]{2,1,0:T(8,128)(2,1)S(1)}, bf16[2,32,256]{2,1,0:T(8,128)(2,1)S(1)}, u32[]{:S(2)}, u32[]{:S(2)}) collective-permute-start(bf16[2,32,256]{2,1,0:T(8,128)(2,1)S(1)} %get-tuple-element.18), channel_id=1, source_target_pairs={{0,24},{4,28},{8,16},{12,20},{16,8},{20,12},{24,0},{28,4},{1,25},{... | collective-permute-start | bytes 98312 | tf_op jit(solution)/shard_map/ppermute | solution.py:207
  12.7 7.9 %collective-permute-start.8 = (bf16[2,32,256]{2,1,0:T(8,128)(2,1)S(1)}, bf16[2,32,256]{2,1,0:T(8,128)(2,1)S(1)}, u32[]{:S(2)}, u32[]{:S(2)}) collective-permute-start(bf16[2,32,256]{2,1,0:T(8,128)(2,1)S(1)} %get-tuple-element.18), channel_id=1, source_target_pairs={{0,20},{4,16},{8,28},{12,24},{16,4},{20,0},{24,12},{28,8},{1,21},{... | collective-permute-start | bytes 98312 | tf_op jit(solution)/shard_map/ppermute | solution.py:207
  14.6 8.3 %collective-permute-start.7 = (bf16[2,32,256]{2,1,0:T(8,128)(2,1)S(1)}, bf16[2,32,256]{2,1,0:T(8,128)(2,1)S(1)}, u32[]{:S(2)}, u32[]{:S(2)}) collective-permute-start(bf16[2,32,256]{2,1,0:T(8,128)(2,1)S(1)} %get-tuple-element.18), channel_id=1, source_target_pairs={{0,16},{4,20},{8,24},{12,28},{16,0},{20,4},{24,8},{28,12},{1,17},{... | collective-permute-start | bytes 98312 | tf_op jit(solution)/shard_map/ppermute | solution.py:207
  16.7 9.1 %collective-permute-start.1 = (bf16[2,128,256]{2,1,0:T(8,128)(2,1)S(1)}, bf16[2,128,256]{2,1,0:T(8,128)(2,1)S(1)}, u32[]{:S(2)}, u32[]{:S(2)}) collective-permute-start(bf16[2,128,256]{2,1,0:T(8,128)(2,1)S(1)} %get-tuple-element.16), channel_id=1, source_target_pairs={{4,8},{8,4},{12,16},{16,12},{20,24},{24,20},{5,9},{9,5},{13,17},{1... | collective-permute-start | bytes 393224 | tf_op jit(solution)/shard_map/ppermute | solution.py:215
  18.3 6.1 %collective-permute-start.2 = (bf16[2,64,256]{2,1,0:T(8,128)(2,1)S(1)}, bf16[2,64,256]{2,1,0:T(8,128)(2,1)S(1)}, u32[]{:S(2)}, u32[]{:S(2)}) collective-permute-start(bf16[2,64,256]{2,1,0:T(8,128)(2,1)S(1)} %get-tuple-element.17), channel_id=1, source_target_pairs={{0,8},{4,12},{8,0},{12,4},{16,24},{20,28},{24,16},{28,20},{1,9},{5... | collective-permute-start | bytes 196616 | tf_op jit(solution)/shard_map/ppermute | solution.py:207
  20.5 5.3 %collective-permute-start.3 = (bf16[2,64,256]{2,1,0:T(8,128)(2,1)S(1)}, bf16[2,64,256]{2,1,0:T(8,128)(2,1)S(1)}, u32[]{:S(2)}, u32[]{:S(2)}) collective-permute-start(bf16[2,64,256]{2,1,0:T(8,128)(2,1)S(1)} %get-tuple-element.17), channel_id=1, source_target_pairs={{0,12},{4,8},{8,4},{12,0},{16,28},{20,24},{24,20},{28,16},{1,13},{... | collective-permute-start | bytes 196616 | tf_op jit(solution)/shard_map/ppermute | solution.py:207
  25.8 1.0 %copy-start.3 = (bf16[1,512,256]{2,1,0:T(8,128)(2,1)S(1)}, bf16[1,512,256]{2,1,0:T(8,128)(2,1)}, u32[]{:S(2)}) copy-start(bf16[1,512,256]{2,1,0:T(8,128)(2,1)} %param.4) | copy-start | bytes 786436
  30.1 1.9 %collective-permute-start.11 = (bf16[128,256]{1,0:T(8,128)(2,1)S(1)}, bf16[128,256]{1,0:T(8,128)(2,1)S(1)}, u32[]{:S(2)}, u32[]{:S(2)}) collective-permute-start(bf16[128,256]{1,0:T(8,128)(2,1)S(1)} %get-tuple-element.20), channel_id=1, source_target_pairs={{0,1},{1,0},{2,3},{3,2},{4,5},{5,4},{6,7},{7,6},{8,9},{9,8},{10,11... | collective-permute-start | bytes 196616 | tf_op jit(solution)/shard_map/ppermute | solution.py:207
  30.2 4.5 %collective-permute-start.12 = (bf16[128,256]{1,0:T(8,128)(2,1)S(1)}, bf16[128,256]{1,0:T(8,128)(2,1)S(1)}, u32[]{:S(2)}, u32[]{:S(2)}) collective-permute-start(bf16[128,256]{1,0:T(8,128)(2,1)S(1)} %get-tuple-element.21), channel_id=1, source_target_pairs={{0,2},{1,3},{2,0},{3,1},{4,6},{5,7},{6,4},{7,5},{8,10},{9,11},{10,... | collective-permute-start | bytes 196616 | tf_op jit(solution)/shard_map/ppermute | solution.py:207
  31.8 4.0 %collective-permute-start.13 = (bf16[128,256]{1,0:T(8,128)(2,1)S(1)}, bf16[128,256]{1,0:T(8,128)(2,1)S(1)}, u32[]{:S(2)}, u32[]{:S(2)}) collective-permute-start(bf16[128,256]{1,0:T(8,128)(2,1)S(1)} %get-tuple-element.22), channel_id=1, source_target_pairs={{0,3},{1,2},{2,1},{3,0},{4,7},{5,6},{6,5},{7,4},{8,11},{9,10},{10,... | collective-permute-start | bytes 196616 | tf_op jit(solution)/shard_map/ppermute | solution.py:207
